TPU v7x, 256 devices: a whole 4x4x8 slice. The times are simulated.
256 devices in a mesh: dp: 4 (over x), segment: 2 (over core), band: 32 (over z, y).
Axes of the slice: x: 4, y: 4, z: 8, core: 2. Of those that a mesh axis runs over, the one named last changes fastest.
Arguments:
- fields: bfloat16 [4, 2, 256, 16, 512], P('dp', None, 'band'), may hold values from -6 to 6
- cell_mask: int32 [4, 2, 256, 16], P('dp', None, 'band'), may hold values 0 or 1
- merge_weight: bfloat16 [2, 1024, 512], P('segment', 'dp'), may hold values from -0.1875 to 0.1875
- qkv_weight: bfloat16 [2, 512, 1536], P('segment', 'dp')
- out_weight: bfloat16 [2, 512, 512], P('segment', 'dp'), may hold values from -1 to 1
- norm_gain: bfloat16 [2, 512], P('segment', 'dp'), may hold values from 0.099609375 to 1.8984375
- out_cotangent: bfloat16 [4, 2, 256, 16, 512], P('dp', None, 'band'), may hold values from -6 to 6
Outputs:
- section_out: bfloat16 [2, 4, 2, 256, 16, 512], P('segment', 'dp', None, 'band')
- merge_grad: float32 [2, 1024, 512], P('segment', 'dp')
- qkv_grad: float32 [2, 512, 1536], P('segment', 'dp')
- out_grad: float32 [2, 512, 512], P('segment', 'dp')
- gain_grad: float32 [2, 512], P('segment', 'dp')
Inputs may be any that keep to these rules, and one draw needn't show every extreme that they name: `cell_mask`: 1 marks a cell whose keys may be attended.
All inputs are finite; a program needn't handle non-finite values. No bound on the sum of `cell_mask` on one device may be relied on, other than what follows from the above.
Results may differ from a plain program's by a relative error of at most 0.03.
Values may be sent and summed in bfloat16 or wider, within the bound.
A program may use at most 128 MiB of HBM per device.

v0:
```python
from functools import partial
import jax
import jax.numpy as jnp
from jax import lax
from jax.sharding import PartitionSpec as P

HEADS = 8
WH = 8
WW = 16
SH = 4
SW = 8
EPSILON = 1e-05
MASKED = -1e30


def padded(shard, sides, width):
    for axis, dim in sides:
        size, length = (lax.axis_size(axis), shard.shape[dim])
        up = [(i, (i + 1) % size) for i in range(size - 1)]
        down = [(j, i) for i, j in up]
        last = lax.slice_in_dim(shard, length - width, length, axis=dim)
        first = lax.slice_in_dim(shard, 0, width, axis=dim)
        before = lax.ppermute(last, axis, up)
        after = lax.ppermute(first, axis, down)
        shard = jnp.concatenate([before, shard, after], axis=dim)
    return shard


def partner(shard, axis, distance):
    return lax.ppermute(shard, axis, [(i, i ^ 1 << distance) for i in range(lax.axis_size(axis))])


def normalize(update):
    average = jnp.mean(update, axis=-1, keepdims=True)
    centered = update - average
    spread = jnp.mean(centered * centered, axis=-1, keepdims=True)
    inverse = lax.rsqrt(spread + EPSILON)
    return (centered * inverse, inverse)


def window_pattern(lon_count):
    query_index = jnp.arange(WH * lon_count, dtype=jnp.int32)
    key_index = jnp.arange(2 * WH * lon_count, dtype=jnp.int32)
    query_row = query_index // lon_count
    query_col = query_index % lon_count
    key_row = key_index // lon_count
    key_col = key_index % lon_count
    lat_same = ((query_row + SH) // WH)[:, None] == (key_row // WH)[None, :]
    lon_same = ((query_col + SW) // WW)[:, None] == ((key_col + SW) // WW)[None, :]
    self_key = ((query_row + SH)[:, None] == key_row[None, :]) & (
        query_col[:, None] == key_col[None, :]
    )
    return (lat_same & lon_same, self_key)


def attend(queries, keyvals, usable):
    row_count, lon_count, feature = queries.shape
    blocks = row_count // WH
    head_dim = feature // HEADS
    query_blocks = queries.reshape(blocks, WH * lon_count, HEADS, head_dim)
    kv_blocks = keyvals.reshape(blocks + 1, WH * lon_count, 2, HEADS, head_dim)
    key_pairs = jnp.concatenate([kv_blocks[:-1], kv_blocks[1:]], axis=1)
    use_blocks = usable.reshape(blocks + 1, WH * lon_count)
    use_pairs = jnp.concatenate([use_blocks[:-1], use_blocks[1:]], axis=1)
    inside, self_key = window_pattern(lon_count)
    allowed = inside[None] & (use_pairs[:, None, :] | self_key[None])
    scores = jnp.einsum(
        "nqhd,nkhd->nhqk", query_blocks, key_pairs[:, :, 0], preferred_element_type=jnp.float32
    ) * head_dim ** (-0.5)
    scores = jnp.where(allowed[:, None], scores, MASKED)
    highest = jnp.max(scores, axis=-1, keepdims=True)
    weights = jnp.exp(scores - highest)
    attn_prob = (weights / jnp.sum(weights, axis=-1, keepdims=True)).astype(jnp.bfloat16)
    mixture = jnp.einsum(
        "nhqk,nkhd->nqhd", attn_prob, key_pairs[:, :, 1], preferred_element_type=jnp.float32
    )
    return mixture.reshape(row_count, lon_count, feature).astype(jnp.bfloat16)


def guarded(active, function, operands):

    def skipped(values):
        return jax.tree.map(jnp.zeros_like, function(values))

    return lax.cond(active, function, skipped, operands)


def project(joined, merge_full, qkv_full, gain_full):
    update = jnp.einsum("rwj,jd->rwd", joined, merge_full, preferred_element_type=jnp.float32)
    normed, inverse = normalize(update)
    hidden = (normed * gain_full.astype(jnp.float32)).astype(jnp.bfloat16)
    projected = jnp.einsum("rwd,de->rwe", hidden, qkv_full, preferred_element_type=jnp.float32)
    feature = update.shape[-1]
    queries = projected[..., :feature].astype(jnp.bfloat16)
    keyvals = projected[..., feature:].astype(jnp.bfloat16)
    return (update, normed, inverse, hidden, queries, keyvals)


def section_forward(active, joined, usable, merge_full, qkv_full, gain_full, out_full):
    update, normed, inverse, hidden, queries, own_keys = guarded(
        active, lambda rows_own: project(rows_own, merge_full, qkv_full, gain_full), joined
    )
    keyvals = padded(own_keys, (("band", 0),), SH)

    def finish(operands):
        update_in, query_in, keyval_in, usable_in = operands
        mixture = attend(query_in, keyval_in, usable_in)
        result = (
            update_in
            + jnp.einsum("rwd,de->rwe", mixture, out_full, preferred_element_type=jnp.float32)
        ).astype(jnp.bfloat16)
        return (mixture, result)

    mixture, result = guarded(active, finish, (update, queries, keyvals, usable))
    return (result, (joined, normed, inverse, hidden, queries, keyvals, mixture))


def attend_back(out_full, operands):
    grad_out, queries, keyvals, mixture, usable = operands
    grad_mixture = jnp.einsum(
        "rwe,de->rwd", grad_out, out_full, preferred_element_type=jnp.float32
    ).astype(jnp.bfloat16)
    unused, pull_back = jax.vjp(
        lambda query_in, keyval_in: attend(query_in, keyval_in, usable), queries, keyvals
    )
    grad_query, grad_keyval = pull_back(grad_mixture)
    grad_outw = jnp.einsum("rwd,rwe->de", mixture, grad_out, preferred_element_type=jnp.float32)
    return (grad_query, grad_keyval, grad_outw)


def fold_rims(grad_keyval, row_count):
    rim_rows = jnp.concatenate([grad_keyval[:SH], grad_keyval[SH + row_count :]], axis=0)
    returned = padded(rim_rows, (("band", 0),), SH)
    own_part = grad_keyval[SH : SH + row_count].astype(jnp.float32)
    return jnp.concatenate(
        [
            own_part[:SH] + returned[:SH].astype(jnp.float32),
            own_part[SH : row_count - SH],
            own_part[row_count - SH :] + returned[3 * SH :].astype(jnp.float32),
        ],
        axis=0,
    ).astype(jnp.bfloat16)


def back_core(qkv_full, gain_full, grad_query, grad_keyown, grad_out, normed, inverse):
    grad_proj = jnp.concatenate([grad_query, grad_keyown], axis=-1)
    grad_hidden = jnp.einsum("rwe,de->rwd", grad_proj, qkv_full, preferred_element_type=jnp.float32)
    grad_normed = grad_hidden * gain_full.astype(jnp.float32)
    grad_update = (
        grad_out.astype(jnp.float32)
        + inverse
        * (
            grad_normed
            - jnp.mean(grad_normed, axis=-1, keepdims=True)
            - normed * jnp.mean(grad_normed * normed, axis=-1, keepdims=True)
        )
    ).astype(jnp.bfloat16)
    return (grad_proj, grad_hidden, grad_update)


def project_back(merge_part, qkv_full, gain_full, operands):
    grad_query, grad_keyown, grad_out, joined, normed, inverse, hidden = operands
    grad_proj, grad_hidden, grad_update = back_core(
        qkv_full, gain_full, grad_query, grad_keyown, grad_out, normed, inverse
    )
    grad_qkv = jnp.einsum("rwd,rwe->de", hidden, grad_proj, preferred_element_type=jnp.float32)
    grad_gain = jnp.sum(grad_hidden * normed, axis=(0, 1))
    grad_merge = jnp.einsum("rwj,rwd->jd", joined, grad_update, preferred_element_type=jnp.float32)
    grad_joined = jnp.einsum(
        "rwd,jd->rwj", grad_update, merge_part, preferred_element_type=jnp.float32
    )
    return (grad_joined, grad_merge, grad_qkv, grad_gain)


def store_slot(buffers, values, slot_index, active):

    def place_one(buffer, new_value):
        current = lax.dynamic_index_in_dim(buffer, slot_index, 0, keepdims=False)
        return lax.dynamic_update_index_in_dim(
            buffer, jnp.where(active, new_value, current), slot_index, 0
        )

    return jax.tree.map(place_one, buffers, values)


def body(fields, cell_mask, merge_weight, qkv_weight, out_weight, norm_gain, out_cotangent):
    merge_rows, qkv_rows, out_rows, gain_rows = (
        lax.all_gather(merge_weight, "dp", axis=1, tiled=True),
        lax.all_gather(qkv_weight, "dp", axis=1, tiled=True),
        lax.all_gather(out_weight, "dp", axis=1, tiled=True),
        lax.all_gather(norm_gain, "dp", axis=1, tiled=True),
    )
    merge_full = merge_rows[0]
    qkv_full = qkv_rows[0]
    out_full = out_rows[0]
    gain_full = gain_rows[0]
    inputs = fields[0]
    cotangent = out_cotangent[0]
    micro_count, row_count, lon_count, feature = inputs.shape
    mask_ext = padded(cell_mask[0], (("band", 1),), SH)
    usable_ext = mask_ext == 1
    section_count = lax.axis_size("segment")
    half_count = section_count // 2
    section_rank = lax.axis_index("segment")
    tick_count = half_count + micro_count - 1

    def to_partner(payload):
        payload = partner(payload, "segment", 0)
        return payload

    def forward_tick(phase, feed):

        def forward_one_tick(tick_index, state_in):
            sending, section_buf, stashed = state_in
            rank_local = section_rank - phase * half_count
            micro_index = tick_index - rank_local
            active = (
                (rank_local >= 0)
                & (rank_local < half_count)
                & (micro_index >= 0)
                & (micro_index < micro_count)
            )
            slot_index = jnp.clip(micro_index, 0, micro_count - 1)
            feed_now = lax.dynamic_index_in_dim(feed, slot_index, 0, keepdims=False)
            joined = jnp.concatenate([feed_now, feed_now], axis=-1)
            usable = lax.dynamic_index_in_dim(usable_ext, slot_index, 0, keepdims=False)
            result, record = section_forward(
                active, joined, usable, merge_full, qkv_full, gain_full, out_full
            )
            section_buf = store_slot(section_buf, result, slot_index, active)
            stashed = store_slot(stashed, record, slot_index, active)
            return (result, section_buf, stashed)

        return forward_one_tick

    def backward_tick(phase, feed, stashed):
        merge_part = merge_full if phase == 0 else merge_full[:feature]

        def backward_one_tick(tick_index, state_in):
            sending, skip_buf, grad_sums = state_in
            rank_local = section_count - 1 - section_rank - phase * half_count
            micro_index = tick_index - rank_local
            active = (
                (rank_local >= 0)
                & (rank_local < half_count)
                & (micro_index >= 0)
                & (micro_index < micro_count)
            )
            slot_index = jnp.clip(micro_index, 0, micro_count - 1)
            grad_out = lax.dynamic_index_in_dim(feed, slot_index, 0, keepdims=False)
            joined, normed, inverse, hidden, queries, keyvals, mixture = jax.tree.map(
                lambda buffer: lax.dynamic_index_in_dim(buffer, slot_index, 0, keepdims=False),
                stashed,
            )
            usable = lax.dynamic_index_in_dim(usable_ext, slot_index, 0, keepdims=False)
            grad_query, grad_keyval, grad_outw = guarded(
                active,
                partial(attend_back, out_full),
                (grad_out, queries, keyvals, mixture, usable),
            )
            grad_keyown = fold_rims(grad_keyval, row_count)
            grad_joined, grad_merge, grad_qkv, grad_gain = guarded(
                active,
                partial(project_back, merge_part, qkv_full, gain_full),
                (grad_query, grad_keyown, grad_out, joined, normed, inverse, hidden),
            )
            grad_sums = (
                grad_sums[0] + grad_merge,
                grad_sums[1] + grad_qkv,
                grad_sums[2] + grad_outw,
                grad_sums[3] + grad_gain,
            )
            grad_chain = grad_joined[..., :feature].astype(jnp.bfloat16)
            if phase == 0:
                grad_side = grad_joined[..., feature:].astype(jnp.bfloat16)
                toward = jnp.where(
                    section_rank == half_count,
                    (grad_chain.astype(jnp.float32) + grad_side.astype(jnp.float32)).astype(
                        jnp.bfloat16
                    ),
                    grad_side,
                )
                skip_buf = store_slot(skip_buf, toward, slot_index, active)
            return (grad_chain, skip_buf, grad_sums)

        return backward_one_tick

    stashed = (
        jnp.zeros((micro_count, row_count, lon_count, 2 * feature), jnp.bfloat16),
        jnp.zeros((micro_count, row_count, lon_count, feature), jnp.float32),
        jnp.zeros((micro_count, row_count, lon_count, 1), jnp.float32),
        jnp.zeros((micro_count, row_count, lon_count, feature), jnp.bfloat16),
        jnp.zeros((micro_count, row_count, lon_count, feature), jnp.bfloat16),
        jnp.zeros((micro_count, row_count + 2 * SH, lon_count, 2 * feature), jnp.bfloat16),
        jnp.zeros((micro_count, row_count, lon_count, feature), jnp.bfloat16),
    )
    section_buf = jnp.zeros((micro_count, row_count, lon_count, feature), jnp.bfloat16)
    spare_rows = jnp.zeros((row_count, lon_count, feature), jnp.bfloat16)
    unused, section_buf, stashed = lax.fori_loop(
        0, tick_count, forward_tick(0, inputs), (spare_rows, section_buf, stashed)
    )
    skip_in = to_partner(section_buf)
    unused, section_buf, stashed = lax.fori_loop(
        0, tick_count, forward_tick(1, skip_in), (spare_rows, section_buf, stashed)
    )
    grad_sums = (
        jnp.zeros((2 * feature, feature), jnp.float32),
        jnp.zeros((feature, 3 * feature), jnp.float32),
        jnp.zeros((feature, feature), jnp.float32),
        jnp.zeros((feature,), jnp.float32),
    )
    unused, skip_buf, grad_sums = lax.fori_loop(
        0,
        tick_count,
        backward_tick(0, cotangent, stashed),
        (spare_rows, jnp.zeros_like(section_buf), grad_sums),
    )
    skip_back = to_partner(skip_buf)
    unused, skip_buf, grad_sums = lax.fori_loop(
        0, tick_count, backward_tick(1, skip_back, stashed), (spare_rows, skip_buf, grad_sums)
    )
    section_home = section_buf[None, None]
    merge_part_sum, qkv_part_sum, out_part_sum, gain_part_sum = (
        lax.psum_scatter(
            grad_sums[0][None].astype(jnp.bfloat16), "dp", scatter_dimension=1, tiled=True
        ).astype(jnp.float32),
        lax.psum_scatter(
            grad_sums[1][None].astype(jnp.bfloat16), "dp", scatter_dimension=1, tiled=True
        ).astype(jnp.float32),
        lax.psum_scatter(
            grad_sums[2][None].astype(jnp.bfloat16), "dp", scatter_dimension=1, tiled=True
        ).astype(jnp.float32),
        lax.psum_scatter(
            grad_sums[3][None].astype(jnp.bfloat16), "dp", scatter_dimension=1, tiled=True
        ).astype(jnp.float32),
    )
    merge_grad, qkv_grad, out_grad, gain_grad = (
        lax.psum(merge_part_sum.astype(jnp.bfloat16), "band").astype(jnp.float32),
        lax.psum(qkv_part_sum.astype(jnp.bfloat16), "band").astype(jnp.float32),
        lax.psum(out_part_sum.astype(jnp.bfloat16), "band").astype(jnp.float32),
        lax.psum(gain_part_sum.astype(jnp.bfloat16), "band").astype(jnp.float32),
    )
    return (section_home, merge_grad, qkv_grad, out_grad, gain_grad)


def solution(mesh):
    return jax.shard_map(
        body,
        mesh=mesh,
        in_specs=(
            P("dp", None, "band", None, None),
            P("dp", None, "band", None),
            P("segment", "dp", None),
            P("segment", "dp", None),
            P("segment", "dp", None),
            P("segment", "dp"),
            P("dp", None, "band", None, None),
        ),
        out_specs=(
            P("segment", "dp", None, "band", None, None),
            P("segment", "dp", None),
            P("segment", "dp", None),
            P("segment", "dp", None),
            P("segment", "dp"),
        ),
        check_vma=False,
    )
```

profile of v0, /device:TPU:2, one launch (start us, length us, event | category | flops | bytes accessed | tf_op | source)
XLA Modules:
  0.0 875.8 jit_solution(191999634789803929)
XLA Ops:
  14.3 13.6 %all_gather.15 = bf16[1,512,512]{2,1,0:T(8,128)(2,1)S(1)} all-gather(bf16[1,128,512]{2,1,0:T(8,128)(2,1)} %param.35), channel_id=1, replica_groups=mesh['dp'=4,'segment'=2,'band'=32] {'dp'}, dimensions={1}, use_global_device_ids=true | all-gather | bytes 655360 | tf_op jit(solution)/shard_map/all_gather | solution.py:190
  27.9 7.6 all_gather.13
  38.2 32.2 %all-gather.5.cloned.1.call-done = bf16[1,512,1536]{2,1,0:T(8,128)(2,1)} async-done(((bf16[1,128,1536]{2,1,0:T(8,128)(2,1)}), bf16[1,512,1536]{2,1,0:T(8,128)(2,1)}) %all-gather.5.cloned.1.call-update) | async-done | bytes 1572880 | tf_op jit(solution)/shard_map/all_gather | solution.py:189
  76.2 116.6 %while.103 = (s32[]{:T(128)}, bf16[2,8,16,512]{3,2,1,0:T(8,128)(2,1)}, bf16[2,8,16,1024]{3,2,1,0:T(8,128)(2,1)}, f32[2,8,16,512]{3,2,1,0:T(8,128)}, f32[2,8,16,1...) while((s32[]{:T(128)}, ...), condition=%wide.region_9.10_spmd, body=%wide.region_0.9_spmd.sunk | while | flops 477448448 | bytes 26721116 | solution.py:299
  77.2 5.2 conditional.18
  84.5 5.2 collective-permute-start.1
  103.1 27.5 %conditional.19 = (bf16[8,16,512]{2,1,0:T(8,128)(2,1)}, bf16[8,16,512]{2,1,0:T(8,128)(2,1)}) conditional(s32[]{:T(128)} %convert_element_type.561, () %tuple.323, (bf16[16,16,1024]{2,1,0:T(8,128)(2,1)}, pred[2,16,16]{2,1,0:T(8,128)(4,1)S(1)}, s32[]{:T(128)}, bf16[8,16,512]{2,1,0:T(8,128)(2,1)S(1)}, bf16[512,512]{1,0:T(8,128)(2,1)S(1)}, ...), branch_computations={%region_5.5_spmd, %region_6.8_spmd} | conditional | flops 137315840 | bytes 8476452 | solution.py:85
  135.4 5.2 conditional.18
  142.7 5.2 collective-permute-start.1
  161.4 27.5 %conditional.19 = (bf16[8,16,512]{2,1,0:T(8,128)(2,1)}, bf16[8,16,512]{2,1,0:T(8,128)(2,1)}) conditional(s32[]{:T(128)} %convert_element_type.561, () %tuple.323, (bf16[16,16,1024]{2,1,0:T(8,128)(2,1)}, pred[2,16,16]{2,1,0:T(8,128)(4,1)S(1)}, s32[]{:T(128)}, bf16[8,16,512]{2,1,0:T(8,128)(2,1)S(1)}, bf16[512,512]{1,0:T(8,128)(2,1)S(1)}, ...), branch_computations={%region_5.5_spmd, %region_6.8_spmd} | conditional | flops 137315840 | bytes 8476452 | solution.py:85
  194.7 54.8 %while.104 = (s32[]{:T(128)}, bf16[2,8,16,512]{3,2,1,0:T(8,128)(2,1)}, bf16[2,8,16,1024]{3,2,1,0:T(8,128)(2,1)}, f32[2,8,16,512]{3,2,1,0:T(8,128)}, f32[2,8,16,1...) while((s32[]{:T(128)}, ...), condition=%wide.region_19.20_spmd, body=%wide.region_10.19_spmd.sunk | while | flops 477448448 | bytes 26721116 | solution.py:303
  199.2 5.2 collective-permute-start.3
  226.6 5.2 collective-permute-start.3
  250.3 60.6 %while.106 = (s32[]{:T(128)}, bf16[2,8,16,512]{3,2,1,0:T(8,128)(2,1)}, f32[1024,512]{1,0:T(8,128)}, f32[512,1536]{1,0:T(8,128)}, f32[512,512]{1,0:T(8,128)}, /*i...) while((s32[]{:T(128)}, ...), condition=%wide.region_33.34_spmd.clone, body=%wide.region_20.33_spmd.clone.sunk | while | flops 992495872 | bytes 121524072 | solution.py:312
  255.1 4.3 collective-permute-start.6
  284.2 6.7 collective-permute-start.6
  303.3 4.3 select_add_fusion.8
  310.9 143.5 %collective-permute-start.11 = (bf16[2,8,16,512]{3,2,1,0:T(8,128)(2,1)}, bf16[2,8,16,512]{3,2,1,0:T(8,128)(2,1)S(1)}, u32[]{:S(2)}, u32[]{:S(2)}) collective-permute-start(bf16[2,8,16,512]{3,2,1,0:T(8,128)(2,1)} %get-tuple-element.2101), channel_id=1, source_target_pairs={{0,32},{32,0},{1,33},{33,1},{2,34},{34,2},{3,35},{35,3},{4,36},{36... | collective-permute-start | bytes 786440 | tf_op jit(solution)/shard_map/ppermute | solution.py:30
  455.8 131.6 %while.105 = (s32[]{:T(128)}, f32[1024,512]{1,0:T(8,128)}, f32[512,1536]{1,0:T(8,128)}, f32[512,512]{1,0:T(8,128)}, f32[512]{0:T(512)}, /*index=5*/s32[]{:T(128)...) while((s32[]{:T(128)}, f32[1024,512]{1,0:T(8,128)}, ...), condition=%wide.region_47.48_spmd, body=%wide.region_34.47_spmd.sunk | while | flops 856311552 | bytes 123788608 | solution.py:319
  456.6 35.0 %conditional.22 = (bf16[8,16,512]{2,1,0:T(8,128)(2,1)}, bf16[16,16,1024]{2,1,0:T(8,128)(2,1)}, f32[512,512]{1,0:T(8,128)}) conditional(s32[]{:T(128)} %convert_element_type.565, () %tuple.339, (pred[2,16,16]{2,1,0:T(8,128)(4,1)S(1)}, s32[]{:T(128)}, bf16[8,16,512]{2,1,0:T(8,128)(2,1)}, bf16[512,512]{1,0:T(8,128)(2,1)S(1)}, ...), branch_computations={%region_35.35_spmd, %region_36.41_spmd} | conditional | flops 316294400 | bytes 26212748 | solution.py:85
  492.6 6.2 collective-permute-start.4
  506.9 6.1 conditional.23
  514.7 4.3 add.947
  522.9 35.0 %conditional.22 = (bf16[8,16,512]{2,1,0:T(8,128)(2,1)}, bf16[16,16,1024]{2,1,0:T(8,128)(2,1)}, f32[512,512]{1,0:T(8,128)}) conditional(s32[]{:T(128)} %convert_element_type.565, () %tuple.339, (pred[2,16,16]{2,1,0:T(8,128)(4,1)S(1)}, s32[]{:T(128)}, bf16[8,16,512]{2,1,0:T(8,128)(2,1)}, bf16[512,512]{1,0:T(8,128)(2,1)S(1)}, ...), branch_computations={%region_35.35_spmd, %region_36.41_spmd} | conditional | flops 316294400 | bytes 26212748 | solution.py:85
  572.2 6.1 conditional.23
  580.0 4.3 add.947
  596.6 27.5 %reduce-scatter.11.cloned.1.call-done = bf16[1,128,512]{2,1,0:T(8,128)(2,1)} async-done(((bf16[1,512,512]{2,1,0:T(8,128)(2,1)}), bf16[1,128,512]{2,1,0:T(8,128)(2,1)}) %reduce-scatter.11.cloned.1.call-update) | async-done | bytes 131088 | tf_op jit(solution)/shard_map/reduce_scatter | solution.py:330
  624.1 28.4 %reduce-scatter.7.cloned.1.call-done = bf16[1,256,512]{2,1,0:T(8,128)(2,1)} async-done(((bf16[1,1024,512]{2,1,0:T(8,128)(2,1)}), bf16[1,256,512]{2,1,0:T(8,128)(2,1)}) %reduce-scatter.7.cloned.1.call-update) | async-done | bytes 262160 | tf_op jit(solution)/shard_map/reduce_scatter | solution.py:324
  652.5 31.1 %reduce-scatter.9.cloned.1.call-done = bf16[1,128,1536]{2,1,0:T(8,128)(2,1)} async-done(((bf16[1,512,1536]{2,1,0:T(8,128)(2,1)}), bf16[1,128,1536]{2,1,0:T(8,128)(2,1)}) %reduce-scatter.9.cloned.1.call-update) | async-done | bytes 393232 | tf_op jit(solution)/shard_map/reduce_scatter | solution.py:327
  683.6 25.3 %reduce-scatter.13.cloned.1.call-done = bf16[128,1]{1,0:T(8,128)(2,1)} async-done(((bf16[512,1]{1,0:T(8,128)(2,1)}), bf16[128,1]{1,0:T(8,128)(2,1)}) %reduce-scatter.13.cloned.1.call-update) | async-done | bytes 272
  709.8 75.3 %psum.31 = bf16[1,128]{1,0:T(2,128)(2,1)S(1)} all-reduce(bf16[1,128]{1,0:T(2,128)(2,1)S(1)} %copy.91), channel_id=1, replica_groups=mesh['dp'=4,'segment'=2,'band'=32] {'band'}, use_global_device_ids=true, to_apply=%region_55.56 | all-reduce | flops 128 | bytes 512 | tf_op jit(solution)/shard_map/psum | solution.py:341
  785.6 77.6 %all-reduce.11.cloned.1.call-done = (bf16[1,256,512]{2,1,0:T(8,128)(2,1)}, bf16[1,128,1536]{2,1,0:T(8,128)(2,1)}, bf16[1,128,512]{2,1,0:T(8,128)(2,1)}) async-done(((bf16[1,256,512]{2,1,0:T(8,128)(2,1)}, bf16[1,128,1536]{2,1,0:T(8,128)(2,1)}, bf16[1,128,512]{2,1,0:T(8,128)(2,1)}), (bf16[1,256,512]{2,1,0:T(8,128)(2,1)}, bf16[1,128,1536]{2,1,0:T(8,128)(2,1)}, ...) | async-done | bytes 786448 | tf_op jit(solution)/shard_map/psum | solution.py:338
  (498 shorter events, 359.9 us)
Async XLA Ops:
  7.2 31.1 %all-gather.3.cloned.1.call-start = ((), (), s32[]{:S(2)}) async-start(), calls=%async_computation.4 | async-start | bytes 1310720 | tf_op jit(solution)/shard_map/all_gather | solution.py:188
  7.9 62.5 %all-gather.5.cloned.1.call-start = ((), (), s32[]{:S(2)}) async-start(), calls=%async_computation.5 | async-start | bytes 1966080 | tf_op jit(solution)/shard_map/all_gather | solution.py:189
  8.6 615.4 %reduce-scatter.11.cloned.1.call-start = ((), (), s32[]{:S(2)}) async-start(), calls=%async_computation.8 | async-start | bytes 655360 | tf_op jit(solution)/shard_map/reduce_scatter | solution.py:330
  9.5 26.0 %collective-permute-start.8 = (s32[2,4,16]{2,1,0:T(4,128)S(1)}, s32[2,4,16]{2,1,0:T(4,128)S(1)}, u32[]{:S(2)}, u32[]{:S(2)}) collective-permute-start(s32[2,4,16]{2,1,0:T(4,128)S(1)} %get-tuple-element.2527), channel_id=1, source_target_pairs={{0,1},{1,2},{2,3},{3,4},{4,5},{5,6},{6,7},{7,8},{8,9},{9,10},{10,1... | collective-permute-start | bytes 1544 | tf_op jit(solution)/shard_map/ppermute | solution.py:23
  12.9 22.5 %collective-permute-start.9 = (s32[2,4,16]{2,1,0:T(4,128)S(1)}, s32[2,4,16]{2,1,0:T(4,128)S(1)}, u32[]{:S(2)}, u32[]{:S(2)}) collective-permute-start(s32[2,4,16]{2,1,0:T(4,128)S(1)} %get-tuple-element.2528), channel_id=1, source_target_pairs={{1,0},{2,1},{3,2},{4,3},{5,4},{6,5},{7,6},{8,7},{9,8},{10,9},{11,1... | collective-permute-start | bytes 1544 | tf_op jit(solution)/shard_map/ppermute | solution.py:24
  38.2 38.0 %copy-start.9 = (bf16[1,1024,512]{2,1,0:T(8,128)(2,1)S(1)}, bf16[1,1024,512]{2,1,0:T(8,128)(2,1)}, u32[]{:S(2)}) copy-start(bf16[1,1024,512]{2,1,0:T(8,128)(2,1)} %all-gather.3.cloned.1.call-done) | copy-start | bytes 3145732
  82.4 16.3 %copy-start.31 = (bf16[2,8,16,512]{3,2,1,0:T(8,128)(2,1)S(1)}, bf16[2,8,16,512]{3,2,1,0:T(8,128)(2,1)}, u32[]{:S(2)}) copy-start(bf16[2,8,16,512]{3,2,1,0:T(8,128)(2,1)} %get-tuple-element.3160) | copy-start | bytes 786436 | tf_op jit(solution)/shard_map/while
  83.2 18.0 %collective-permute-start = (bf16[4,16,1024]{2,1,0:T(8,128)(2,1)}, bf16[4,16,1024]{2,1,0:T(8,128)(2,1)}, u32[]{:S(2)}, u32[]{:S(2)}) collective-permute-start(bf16[4,16,1024]{2,1,0:T(8,128)(2,1)} %get-tuple-element.2975), channel_id=1, source_target_pairs={{1,0},{2,1},{3,2},{4,3},{5,4},{6,5},{7,6},{8,7},{9,8},{10,9},{11,1... | collective-permute-start | bytes 393224 | tf_op jit(solution)/shard_map/while/body/eval_jaxpr/ppermute | solution.py:24
  84.5 16.8 %collective-permute-start.1 = (bf16[4,16,1024]{2,1,0:T(8,128)(2,1)}, bf16[4,16,1024]{2,1,0:T(8,128)(2,1)}, u32[]{:S(2)}, u32[]{:S(2)}) collective-permute-start(bf16[4,16,1024]{2,1,0:T(8,128)(2,1)} %get-tuple-element.2976), channel_id=1, source_target_pairs={{0,1},{1,2},{2,3},{3,4},{4,5},{5,6},{6,7},{7,8},{8,9},{9,10},{10,1... | collective-permute-start | bytes 393224 | tf_op jit(solution)/shard_map/while/body/eval_jaxpr/ppermute | solution.py:23
  140.7 16.3 %copy-start.31 = (bf16[2,8,16,512]{3,2,1,0:T(8,128)(2,1)S(1)}, bf16[2,8,16,512]{3,2,1,0:T(8,128)(2,1)}, u32[]{:S(2)}) copy-start(bf16[2,8,16,512]{3,2,1,0:T(8,128)(2,1)} %get-tuple-element.3160) | copy-start | bytes 786436 | tf_op jit(solution)/shard_map/while
  141.5 18.0 %collective-permute-start = (bf16[4,16,1024]{2,1,0:T(8,128)(2,1)}, bf16[4,16,1024]{2,1,0:T(8,128)(2,1)}, u32[]{:S(2)}, u32[]{:S(2)}) collective-permute-start(bf16[4,16,1024]{2,1,0:T(8,128)(2,1)} %get-tuple-element.2975), channel_id=1, source_target_pairs={{1,0},{2,1},{3,2},{4,3},{5,4},{6,5},{7,6},{8,7},{9,8},{10,9},{11,1... | collective-permute-start | bytes 393224 | tf_op jit(solution)/shard_map/while/body/eval_jaxpr/ppermute | solution.py:24
  142.7 16.8 %collective-permute-start.1 = (bf16[4,16,1024]{2,1,0:T(8,128)(2,1)}, bf16[4,16,1024]{2,1,0:T(8,128)(2,1)}, u32[]{:S(2)}, u32[]{:S(2)}) collective-permute-start(bf16[4,16,1024]{2,1,0:T(8,128)(2,1)} %get-tuple-element.2976), channel_id=1, source_target_pairs={{0,1},{1,2},{2,3},{3,4},{4,5},{5,6},{6,7},{7,8},{8,9},{9,10},{10,1... | collective-permute-start | bytes 393224 | tf_op jit(solution)/shard_map/while/body/eval_jaxpr/ppermute | solution.py:23
  192.8 1.9 collective-permute-start.10
  197.9 17.1 %collective-permute-start.2 = (bf16[4,16,1024]{2,1,0:T(8,128)(2,1)}, bf16[4,16,1024]{2,1,0:T(8,128)(2,1)}, u32[]{:S(2)}, u32[]{:S(2)}) collective-permute-start(bf16[4,16,1024]{2,1,0:T(8,128)(2,1)} %get-tuple-element.3006), channel_id=1, source_target_pairs={{1,0},{2,1},{3,2},{4,3},{5,4},{6,5},{7,6},{8,7},{9,8},{10,9},{11,1... | collective-permute-start | bytes 393224 | tf_op jit(solution)/shard_map/while/body/eval_jaxpr/ppermute | solution.py:24
  199.2 15.8 %collective-permute-start.3 = (bf16[4,16,1024]{2,1,0:T(8,128)(2,1)}, bf16[4,16,1024]{2,1,0:T(8,128)(2,1)}, u32[]{:S(2)}, u32[]{:S(2)}) collective-permute-start(bf16[4,16,1024]{2,1,0:T(8,128)(2,1)} %get-tuple-element.3007), channel_id=1, source_target_pairs={{0,1},{1,2},{2,3},{3,4},{4,5},{5,6},{6,7},{7,8},{8,9},{9,10},{10,1... | collective-permute-start | bytes 393224 | tf_op jit(solution)/shard_map/while/body/eval_jaxpr/ppermute | solution.py:23
  225.3 17.1 %collective-permute-start.2 = (bf16[4,16,1024]{2,1,0:T(8,128)(2,1)}, bf16[4,16,1024]{2,1,0:T(8,128)(2,1)}, u32[]{:S(2)}, u32[]{:S(2)}) collective-permute-start(bf16[4,16,1024]{2,1,0:T(8,128)(2,1)} %get-tuple-element.3006), channel_id=1, source_target_pairs={{1,0},{2,1},{3,2},{4,3},{5,4},{6,5},{7,6},{8,7},{9,8},{10,9},{11,1... | collective-permute-start | bytes 393224 | tf_op jit(solution)/shard_map/while/body/eval_jaxpr/ppermute | solution.py:24
  226.6 15.8 %collective-permute-start.3 = (bf16[4,16,1024]{2,1,0:T(8,128)(2,1)}, bf16[4,16,1024]{2,1,0:T(8,128)(2,1)}, u32[]{:S(2)}, u32[]{:S(2)}) collective-permute-start(bf16[4,16,1024]{2,1,0:T(8,128)(2,1)} %get-tuple-element.3007), channel_id=1, source_target_pairs={{0,1},{1,2},{2,3},{3,4},{4,5},{5,6},{6,7},{7,8},{8,9},{9,10},{10,1... | collective-permute-start | bytes 393224 | tf_op jit(solution)/shard_map/while/body/eval_jaxpr/ppermute | solution.py:23
  255.1 11.4 %collective-permute-start.6 = (bf16[4,16,1024]{2,1,0:T(8,128)(2,1)}, bf16[4,16,1024]{2,1,0:T(8,128)(2,1)}, u32[]{:S(2)}, u32[]{:S(2)}) collective-permute-start(bf16[4,16,1024]{2,1,0:T(8,128)(2,1)} %get-tuple-element.3072), channel_id=1, source_target_pairs={{0,1},{1,2},{2,3},{3,4},{4,5},{5,6},{6,7},{7,8},{8,9},{9,10},{10,1... | collective-permute-start | bytes 393224 | tf_op jit(solution)/shard_map/while/body/eval_jaxpr/ppermute | solution.py:23
  259.4 8.4 collective-permute-start.7
  284.2 14.1 %collective-permute-start.6 = (bf16[4,16,1024]{2,1,0:T(8,128)(2,1)}, bf16[4,16,1024]{2,1,0:T(8,128)(2,1)}, u32[]{:S(2)}, u32[]{:S(2)}) collective-permute-start(bf16[4,16,1024]{2,1,0:T(8,128)(2,1)} %get-tuple-element.3072), channel_id=1, source_target_pairs={{0,1},{1,2},{2,3},{3,4},{4,5},{5,6},{6,7},{7,8},{8,9},{9,10},{10,1... | collective-permute-start | bytes 393224 | tf_op jit(solution)/shard_map/while/body/eval_jaxpr/ppermute | solution.py:23
  290.9 7.4 collective-permute-start.7
  310.9 144.9 %collective-permute-start.11 = (bf16[2,8,16,512]{3,2,1,0:T(8,128)(2,1)}, bf16[2,8,16,512]{3,2,1,0:T(8,128)(2,1)S(1)}, u32[]{:S(2)}, u32[]{:S(2)}) collective-permute-start(bf16[2,8,16,512]{3,2,1,0:T(8,128)(2,1)} %get-tuple-element.2101), channel_id=1, source_target_pairs={{0,32},{32,0},{1,33},{33,1},{2,34},{34,2},{3,35},{35,3},{4,36},{36... | collective-permute-start | bytes 786440 | tf_op jit(solution)/shard_map/ppermute | solution.py:30
  456.6 43.5 %copy-start.10 = (f32[512,512]{1,0:T(8,128)S(1)}, f32[512,512]{1,0:T(8,128)}, u32[]{:S(2)}) copy-start(f32[512,512]{1,0:T(8,128)} %get-tuple-element.3359) | copy-start | bytes 3145732 | tf_op jit(solution)/shard_map/while
  492.6 10.3 %collective-permute-start.4 = (bf16[4,16,1024]{2,1,0:T(8,128)(2,1)S(1)}, bf16[4,16,1024]{2,1,0:T(8,128)(2,1)}, u32[]{:S(2)}, u32[]{:S(2)}) collective-permute-start(bf16[4,16,1024]{2,1,0:T(8,128)(2,1)S(1)} %get-tuple-element.3040), channel_id=1, source_target_pairs={{0,1},{1,2},{2,3},{3,4},{4,5},{5,6},{6,7},{7,8},{8,9},{9,10},{10,1... | collective-permute-start | bytes 393224 | tf_op jit(solution)/shard_map/while/body/eval_jaxpr/ppermute | solution.py:23
  498.8 7.0 collective-permute-start.5
  522.9 41.3 %copy-start.10 = (f32[512,512]{1,0:T(8,128)S(1)}, f32[512,512]{1,0:T(8,128)}, u32[]{:S(2)}) copy-start(f32[512,512]{1,0:T(8,128)} %get-tuple-element.3359) | copy-start | bytes 3145732 | tf_op jit(solution)/shard_map/while
  558.9 8.2 collective-permute-start.4
  562.9 8.1 collective-permute-start.5
  589.5 62.9 %reduce-scatter.7.cloned.1.call-start = ((), (), s32[]{:S(2)}) async-start(), calls=%async_computation.6 | async-start | bytes 1310720 | tf_op jit(solution)/shard_map/reduce_scatter | solution.py:324
  592.4 91.3 %reduce-scatter.9.cloned.1.call-start = ((), (), s32[]{:S(2)}) async-start(), calls=%async_computation.7 | async-start | bytes 1966080 | tf_op jit(solution)/shard_map/reduce_scatter | solution.py:327
  595.7 113.3 %reduce-scatter.13.cloned.1.call-start = ((), (), s32[]{:S(2)}) async-start(), calls=%async_computation.9 | async-start | bytes 163840
  596.5 266.7 %all-reduce.11.cloned.1.call-start = ((), (), s32[]{:S(2)}) async-start(), calls=%async_computation.10 | async-start | bytes 1572864 | tf_op jit(solution)/shard_map/psum | solution.py:338
  (64 other events, 277.0 us)
Sparse Core Ops, SparseCore 0:
  9.8 28.3 all-gather.2
  40.0 30.3 all-gather.4
  589.7 34.3 reduce-scatter.10
  626.5 25.9 reduce-scatter.6
  655.0 28.5 reduce-scatter.8
  686.7 22.2 reduce-scatter.12
  712.6 150.6 all-reduce.10
where the time goes:
time: 888 us; the launch traced here: 876 us
  waiting for transfers between devices  237 us (27%)
  starting transfers between devices  201 us (23%)
  local copies, waits for them, and re-layouts  166 us (19%)
  other arithmetic  116 us (13%)
  blocking collectives  96.5 us (11%)
  matrix products  42.6 us (5%)
  between operations  14.6 us (2%)
    ppermute x2, starting transfers between devices, partner(): lax.ppermute(shard, axis, [(i, i ^ 1 << distance) for i in range(lax.axis...  144 us
    psum x1, waiting for transfers between devices, body(): lax.psum(merge_part_sum.astype(jnp.bfloat16), 'band').astype(jnp.float32)  77.6 us
    psum x1, blocking collectives, body(): lax.psum(gain_part_sum.astype(jnp.bfloat16), 'band').astype(jnp.float32)  75.3 us
    ppermute x9, starting transfers between devices, padded(): before = lax.ppermute(last, axis, up)  45.6 us
    slice x20, local copies, waits for them, and re-layouts, attend(): key_pairs = jnp.concatenate([kv_blocks[:-1], kv_blocks[1:]], axis=1)  38.4 us
    all_gather x1, waiting for transfers between devices, body(): lax.all_gather(qkv_weight, 'dp', axis=1, tiled=True)  32.2 us
    reduce_scatter x1, waiting for transfers between devices, body(): lax.psum_scatter(grad_sums[1][None].astype(jnp.bfloat16), 'dp', scatter_d...  31.1 us
    dynamic_update_slice x26, other arithmetic, place_one(): lax.dynamic_update_index_in_dim(buffer, jnp.where(active, new_value, curr...  30.9 us
  transfers between devices with their start and end apart: 27, of which 12 were waited for; matrix products, arithmetic and copies ran while one was open for 8% of the time, Pallas kernels for 0%

commit v1 on v0

--- a/solution.py
+++ b/solution.py
@@ -11,6 +11,24 @@
 SW = 8
 EPSILON = 1e-05
 MASKED = -1e30
+
+
+def collect(shard, axis, dim):
+    ways, here, lap = (lax.axis_size(axis), lax.axis_index(axis), shard.shape[dim])
+    dims = [n * ways if d == dim else n for d, n in enumerate(shard.shape)]
+    full = lax.dynamic_update_slice_in_dim(
+        jnp.zeros(dims, shard.dtype), shard, here * lap, axis=dim
+    )
+    going_up = going_down = shard
+    for far in range(1, ways // 2 + 1):
+        going_up = lax.ppermute(going_up, axis, [(d, (d + 1) % ways) for d in range(ways)])
+        full = lax.dynamic_update_slice_in_dim(full, going_up, (here - far) % ways * lap, axis=dim)
+        if 2 * far < ways:
+            going_down = lax.ppermute(going_down, axis, [(d, (d - 1) % ways) for d in range(ways)])
+            full = lax.dynamic_update_slice_in_dim(
+                full, going_down, (here + far) % ways * lap, axis=dim
+            )
+    return full
 
 
 def padded(shard, sides, width):
@@ -186,7 +204,7 @@
 def body(fields, cell_mask, merge_weight, qkv_weight, out_weight, norm_gain, out_cotangent):
     merge_rows, qkv_rows, out_rows, gain_rows = (
         lax.all_gather(merge_weight, "dp", axis=1, tiled=True),
-        lax.all_gather(qkv_weight, "dp", axis=1, tiled=True),
+        collect(qkv_weight, "dp", 1),
         lax.all_gather(out_weight, "dp", axis=1, tiled=True),
         lax.all_gather(norm_gain, "dp", axis=1, tiled=True),
     )

time: 888 us -> 878 us (0.989)
  waiting for transfers between devices: 237 us -> 214 us
  starting transfers between devices: 201 us -> 216 us
    all_gather x1 -> x0, waiting for transfers between devices: 32.2 us -> none  [body(): lax.all_gather(qkv_weight, 'dp', axis=1, tiled=True)]
    ppermute x2, starting transfers between devices: 144 us -> 155 us  [partner(): lax.ppermute(shard, axis, [(i, i ^ 1 << distance) for i in range(lax.axis...]
    unnamed x8 -> x7, waiting for transfers between devices: 26.8 us -> 25.5 us
  transfers between devices with their start and end apart: 27 -> 29, of which waited for: 12 -> 11; matrix products, arithmetic and copies ran while one was open for 8% -> 8% of each run, Pallas kernels for 0% -> 0%
where the time goes in v1:
time: 878 us; the launch traced here: 867 us
  starting transfers between devices  216 us (25%)
  waiting for transfers between devices  214 us (24%)
  local copies, waits for them, and re-layouts  166 us (19%)
  other arithmetic  113 us (13%)
  blocking collectives  98.4 us (11%)
  matrix products  42.6 us (5%)
  between operations  14.8 us (2%)
    ppermute x2, starting transfers between devices, partner(): lax.ppermute(shard, axis, [(i, i ^ 1 << distance) for i in range(lax.axis...  155 us
    psum x1, waiting for transfers between devices, body(): lax.psum(merge_part_sum.astype(jnp.bfloat16), 'band').astype(jnp.float32)  77.5 us
    psum x1, blocking collectives, body(): lax.psum(gain_part_sum.astype(jnp.bfloat16), 'band').astype(jnp.float32)  75.2 us
    ppermute x9, starting transfers between devices, padded(): before = lax.ppermute(last, axis, up)  45.8 us
    slice x20, local copies, waits for them, and re-layouts, attend(): key_pairs = jnp.concatenate([kv_blocks[:-1], kv_blocks[1:]], axis=1)  38.3 us
    reduce_scatter x1, waiting for transfers between devices, body(): lax.psum_scatter(grad_sums[2][None].astype(jnp.bfloat16), 'dp', scatter_d...  32.4 us
    reduce_scatter x1, waiting for transfers between devices, body(): lax.psum_scatter(grad_sums[1][None].astype(jnp.bfloat16), 'dp', scatter_d...  31.1 us
    dynamic_update_slice x26, other arithmetic, place_one(): lax.dynamic_update_index_in_dim(buffer, jnp.where(active, new_value, curr...  30.9 us
  transfers between devices with their start and end apart: 29, of which 11 were waited for; matrix products, arithmetic and copies ran while one was open for 8% of the time, Pallas kernels for 0%

profile of v1, /device:TPU:2, one launch (start us, length us, event | category | flops | bytes accessed | tf_op | source)
XLA Modules:
  0.0 867.3 jit_solution(7019949298210601107)
XLA Ops:
  15.2 14.8 %all_gather.11 = bf16[1,512,512]{2,1,0:T(8,128)(2,1)S(1)} all-gather(bf16[1,128,512]{2,1,0:T(8,128)(2,1)S(1)} %copy-done.44), channel_id=1, replica_groups=mesh['dp'=4,'segment'=2,'band'=32] {'dp'}, dimensions={1}, use_global_device_ids=true | all-gather | bytes 655360 | tf_op jit(solution)/shard_map/all_gather | solution.py:208
  30.0 8.4 all_gather.10
  39.2 7.8 collective-permute-done.10
  52.8 116.4 %while.103 = (s32[]{:T(128)}, bf16[2,8,16,512]{3,2,1,0:T(8,128)(2,1)}, bf16[2,8,16,1024]{3,2,1,0:T(8,128)(2,1)}, f32[2,8,16,512]{3,2,1,0:T(8,128)}, f32[2,8,16,1...) while((s32[]{:T(128)}, ...), condition=%wide.region_9.10_spmd, body=%wide.region_0.9_spmd.sunk | while | flops 477448448 | bytes 26721116 | solution.py:317
  53.8 5.3 conditional.18
  61.1 5.2 collective-permute-start.1
  79.6 27.4 %conditional.19 = (bf16[8,16,512]{2,1,0:T(8,128)(2,1)}, bf16[8,16,512]{2,1,0:T(8,128)(2,1)}) conditional(s32[]{:T(128)} %convert_element_type.561, () %tuple.323, (bf16[16,16,1024]{2,1,0:T(8,128)(2,1)}, pred[2,16,16]{2,1,0:T(8,128)(4,1)S(1)}, s32[]{:T(128)}, bf16[8,16,512]{2,1,0:T(8,128)(2,1)S(1)}, bf16[512,512]{1,0:T(8,128)(2,1)S(1)}, ...), branch_computations={%region_5.5_spmd, %region_6.8_spmd} | conditional | flops 137315840 | bytes 8476452 | solution.py:103
  111.9 5.3 conditional.18
  119.3 5.2 collective-permute-start.1
  137.8 27.4 %conditional.19 = (bf16[8,16,512]{2,1,0:T(8,128)(2,1)}, bf16[8,16,512]{2,1,0:T(8,128)(2,1)}) conditional(s32[]{:T(128)} %convert_element_type.561, () %tuple.323, (bf16[16,16,1024]{2,1,0:T(8,128)(2,1)}, pred[2,16,16]{2,1,0:T(8,128)(4,1)S(1)}, s32[]{:T(128)}, bf16[8,16,512]{2,1,0:T(8,128)(2,1)S(1)}, bf16[512,512]{1,0:T(8,128)(2,1)S(1)}, ...), branch_computations={%region_5.5_spmd, %region_6.8_spmd} | conditional | flops 137315840 | bytes 8476452 | solution.py:103
  169.2 12.2 %collective-permute-start.13 = (bf16[2,8,16,512]{3,2,1,0:T(8,128)(2,1)}, bf16[2,8,16,512]{3,2,1,0:T(8,128)(2,1)}, u32[]{:S(2)}, u32[]{:S(2)}) collective-permute-start(bf16[2,8,16,512]{3,2,1,0:T(8,128)(2,1)} %get-tuple-element.3200), channel_id=1, source_target_pairs={{0,32},{32,0},{1,33},{33,1},{2,34},{34,2},{3,35},{35,3},{4,36},{36... | collective-permute-start | bytes 786440 | tf_op jit(solution)/shard_map/ppermute | solution.py:48
  183.3 54.9 %while.104 = (s32[]{:T(128)}, bf16[2,8,16,512]{3,2,1,0:T(8,128)(2,1)}, bf16[2,8,16,1024]{3,2,1,0:T(8,128)(2,1)}, f32[2,8,16,512]{3,2,1,0:T(8,128)}, f32[2,8,16,1...) while((s32[]{:T(128)}, ...), condition=%wide.region_19.20_spmd, body=%wide.region_10.19_spmd.sunk | while | flops 477448448 | bytes 26721116 | solution.py:321
  187.8 5.2 collective-permute-start.3
  215.2 5.2 collective-permute-start.3
  238.9 60.7 %while.106 = (s32[]{:T(128)}, bf16[2,8,16,512]{3,2,1,0:T(8,128)(2,1)}, f32[1024,512]{1,0:T(8,128)}, f32[512,1536]{1,0:T(8,128)}, f32[512,512]{1,0:T(8,128)}, /*i...) while((s32[]{:T(128)}, ...), condition=%wide.region_33.34_spmd.clone, body=%wide.region_20.33_spmd.clone.sunk | while | flops 992495872 | bytes 121524072 | solution.py:330
  243.5 4.8 collective-permute-start.6
  273.1 6.7 collective-permute-start.6
  292.1 4.3 select_add_fusion.8
  299.6 143.2 %collective-permute-start.14 = (bf16[2,8,16,512]{3,2,1,0:T(8,128)(2,1)}, bf16[2,8,16,512]{3,2,1,0:T(8,128)(2,1)S(1)}, u32[]{:S(2)}, u32[]{:S(2)}) collective-permute-start(bf16[2,8,16,512]{3,2,1,0:T(8,128)(2,1)} %get-tuple-element.2101), channel_id=1, source_target_pairs={{0,32},{32,0},{1,33},{33,1},{2,34},{34,2},{3,35},{35,3},{4,36},{36... | collective-permute-start | bytes 786440 | tf_op jit(solution)/shard_map/ppermute | solution.py:48
  444.2 131.4 %while.105 = (s32[]{:T(128)}, f32[1024,512]{1,0:T(8,128)}, f32[512,1536]{1,0:T(8,128)}, f32[512,512]{1,0:T(8,128)}, f32[512]{0:T(512)}, /*index=5*/s32[]{:T(128)...) while((s32[]{:T(128)}, f32[1024,512]{1,0:T(8,128)}, ...), condition=%wide.region_47.48_spmd, body=%wide.region_34.47_spmd.sunk | while | flops 856311552 | bytes 123788608 | solution.py:337
  445.0 34.9 %conditional.22 = (bf16[8,16,512]{2,1,0:T(8,128)(2,1)}, bf16[16,16,1024]{2,1,0:T(8,128)(2,1)}, f32[512,512]{1,0:T(8,128)}) conditional(s32[]{:T(128)} %convert_element_type.565, () %tuple.339, (pred[2,16,16]{2,1,0:T(8,128)(4,1)S(1)}, s32[]{:T(128)}, bf16[8,16,512]{2,1,0:T(8,128)(2,1)}, bf16[512,512]{1,0:T(8,128)(2,1)S(1)}, ...), branch_computations={%region_35.35_spmd, %region_36.41_spmd} | conditional | flops 316294400 | bytes 26212748 | solution.py:103
  480.9 6.2 collective-permute-start.4
  495.2 6.1 conditional.23
  503.0 4.3 add.982
  511.2 34.9 %conditional.22 = (bf16[8,16,512]{2,1,0:T(8,128)(2,1)}, bf16[16,16,1024]{2,1,0:T(8,128)(2,1)}, f32[512,512]{1,0:T(8,128)}) conditional(s32[]{:T(128)} %convert_element_type.565, () %tuple.339, (pred[2,16,16]{2,1,0:T(8,128)(4,1)S(1)}, s32[]{:T(128)}, bf16[8,16,512]{2,1,0:T(8,128)(2,1)}, bf16[512,512]{1,0:T(8,128)(2,1)S(1)}, ...), branch_computations={%region_35.35_spmd, %region_36.41_spmd} | conditional | flops 316294400 | bytes 26212748 | solution.py:103
  560.4 6.1 conditional.23
  583.1 32.4 %reduce-scatter.11.cloned.1.call-done = bf16[1,128,512]{2,1,0:T(8,128)(2,1)} async-done(((bf16[1,512,512]{2,1,0:T(8,128)(2,1)}), bf16[1,128,512]{2,1,0:T(8,128)(2,1)}) %reduce-scatter.11.cloned.1.call-update) | async-done | bytes 131088 | tf_op jit(solution)/shard_map/reduce_scatter | solution.py:348
  615.5 28.5 %reduce-scatter.7.cloned.1.call-done = bf16[1,256,512]{2,1,0:T(8,128)(2,1)} async-done(((bf16[1,1024,512]{2,1,0:T(8,128)(2,1)}), bf16[1,256,512]{2,1,0:T(8,128)(2,1)}) %reduce-scatter.7.cloned.1.call-update) | async-done | bytes 262160 | tf_op jit(solution)/shard_map/reduce_scatter | solution.py:342
  644.1 31.1 %reduce-scatter.9.cloned.1.call-done = bf16[1,128,1536]{2,1,0:T(8,128)(2,1)} async-done(((bf16[1,512,1536]{2,1,0:T(8,128)(2,1)}), bf16[1,128,1536]{2,1,0:T(8,128)(2,1)}) %reduce-scatter.9.cloned.1.call-update) | async-done | bytes 393232 | tf_op jit(solution)/shard_map/reduce_scatter | solution.py:345
  675.2 25.4 %reduce-scatter.13.cloned.1.call-done = bf16[128,1]{1,0:T(8,128)(2,1)} async-done(((bf16[512,1]{1,0:T(8,128)(2,1)}), bf16[128,1]{1,0:T(8,128)(2,1)}) %reduce-scatter.13.cloned.1.call-update) | async-done | bytes 272
  701.4 75.2 %psum.31 = bf16[1,128]{1,0:T(2,128)(2,1)S(1)} all-reduce(bf16[1,128]{1,0:T(2,128)(2,1)S(1)} %copy.91), channel_id=1, replica_groups=mesh['dp'=4,'segment'=2,'band'=32] {'band'}, use_global_device_ids=true, to_apply=%region_55.56 | all-reduce | flops 128 | bytes 512 | tf_op jit(solution)/shard_map/psum | solution.py:359
  777.1 77.5 %all-reduce.11.cloned.1.call-done = (bf16[1,256,512]{2,1,0:T(8,128)(2,1)}, bf16[1,128,1536]{2,1,0:T(8,128)(2,1)}, bf16[1,128,512]{2,1,0:T(8,128)(2,1)}) async-done(((bf16[1,256,512]{2,1,0:T(8,128)(2,1)}, bf16[1,128,1536]{2,1,0:T(8,128)(2,1)}, bf16[1,128,512]{2,1,0:T(8,128)(2,1)}), (bf16[1,256,512]{2,1,0:T(8,128)(2,1)}, bf16[1,128,1536]{2,1,0:T(8,128)(2,1)}, ...) | async-done | bytes 786448 | tf_op jit(solution)/shard_map/psum | solution.py:356
  (514 shorter events, 360.9 us)
Async XLA Ops:
  7.2 31.2 %copy-start.45 = (s32[1,2,8,16]{3,2,1,0:T(8,128)S(1)}, s32[1,2,8,16]{3,2,1,0:T(8,128)}, u32[]{:S(2)}) copy-start(s32[1,2,8,16]{3,2,1,0:T(8,128)} %param.32) | copy-start | bytes 3076
  7.2 39.8 %all-gather.2.cloned.1.call-start = ((), (), s32[]{:S(2)}) async-start(), calls=%async_computation.4 | async-start | bytes 1310720 | tf_op jit(solution)/shard_map/all_gather | solution.py:206
  7.3 31.9 %collective-permute-start.9 = (bf16[1,128,1536]{2,1,0:T(8,128)(2,1)}, bf16[1,128,1536]{2,1,0:T(8,128)(2,1)S(1)}, u32[]{:S(2)}, u32[]{:S(2)}) collective-permute-start(bf16[1,128,1536]{2,1,0:T(8,128)(2,1)} %param.34), channel_id=1, source_target_pairs={{0,192},{64,0},{128,64},{192,128},{1,193},{65,1},{129,65},{193,129... | collective-permute-start | bytes 1179656 | tf_op jit(solution)/shard_map/ppermute | solution.py:27
  9.6 28.8 %collective-permute-start.8 = (bf16[1,128,1536]{2,1,0:T(8,128)(2,1)}, bf16[1,128,1536]{2,1,0:T(8,128)(2,1)S(1)}, u32[]{:S(2)}, u32[]{:S(2)}) collective-permute-start(bf16[1,128,1536]{2,1,0:T(8,128)(2,1)} %param.34), channel_id=1, source_target_pairs={{0,64},{64,128},{128,192},{192,0},{1,65},{65,129},{129,193},{193,1... | collective-permute-start | bytes 1179656 | tf_op jit(solution)/shard_map/ppermute | solution.py:24
  9.6 605.9 %reduce-scatter.11.cloned.1.call-start = ((), (), s32[]{:S(2)}) async-start(), calls=%async_computation.7 | async-start | bytes 655360 | tf_op jit(solution)/shard_map/reduce_scatter | solution.py:348
  10.5 27.9 %collective-permute-start.11 = (s32[2,4,16]{2,1,0:T(4,128)S(1)}, s32[2,4,16]{2,1,0:T(4,128)S(1)}, u32[]{:S(2)}, u32[]{:S(2)}) collective-permute-start(s32[2,4,16]{2,1,0:T(4,128)S(1)} %get-tuple-element.2527), channel_id=1, source_target_pairs={{0,1},{1,2},{2,3},{3,4},{4,5},{5,6},{6,7},{7,8},{8,9},{9,10},{10,1... | collective-permute-start | bytes 1544 | tf_op jit(solution)/shard_map/ppermute | solution.py:41
  13.7 24.7 %collective-permute-start.12 = (s32[2,4,16]{2,1,0:T(4,128)S(1)}, s32[2,4,16]{2,1,0:T(4,128)S(1)}, u32[]{:S(2)}, u32[]{:S(2)}) collective-permute-start(s32[2,4,16]{2,1,0:T(4,128)S(1)} %get-tuple-element.2528), channel_id=1, source_target_pairs={{1,0},{2,1},{3,2},{4,3},{5,4},{6,5},{7,6},{8,7},{9,8},{10,9},{11,1... | collective-permute-start | bytes 1544 | tf_op jit(solution)/shard_map/ppermute | solution.py:42
  38.4 8.5 collective-permute-start.10
  59.8 18.0 %collective-permute-start = (bf16[4,16,1024]{2,1,0:T(8,128)(2,1)}, bf16[4,16,1024]{2,1,0:T(8,128)(2,1)}, u32[]{:S(2)}, u32[]{:S(2)}) collective-permute-start(bf16[4,16,1024]{2,1,0:T(8,128)(2,1)} %get-tuple-element.2975), channel_id=1, source_target_pairs={{1,0},{2,1},{3,2},{4,3},{5,4},{6,5},{7,6},{8,7},{9,8},{10,9},{11,1... | collective-permute-start | bytes 393224 | tf_op jit(solution)/shard_map/while/body/eval_jaxpr/ppermute | solution.py:42
  61.1 16.7 %collective-permute-start.1 = (bf16[4,16,1024]{2,1,0:T(8,128)(2,1)}, bf16[4,16,1024]{2,1,0:T(8,128)(2,1)}, u32[]{:S(2)}, u32[]{:S(2)}) collective-permute-start(bf16[4,16,1024]{2,1,0:T(8,128)(2,1)} %get-tuple-element.2976), channel_id=1, source_target_pairs={{0,1},{1,2},{2,3},{3,4},{4,5},{5,6},{6,7},{7,8},{8,9},{9,10},{10,1... | collective-permute-start | bytes 393224 | tf_op jit(solution)/shard_map/while/body/eval_jaxpr/ppermute | solution.py:41
  118.0 18.0 %collective-permute-start = (bf16[4,16,1024]{2,1,0:T(8,128)(2,1)}, bf16[4,16,1024]{2,1,0:T(8,128)(2,1)}, u32[]{:S(2)}, u32[]{:S(2)}) collective-permute-start(bf16[4,16,1024]{2,1,0:T(8,128)(2,1)} %get-tuple-element.2975), channel_id=1, source_target_pairs={{1,0},{2,1},{3,2},{4,3},{5,4},{6,5},{7,6},{8,7},{9,8},{10,9},{11,1... | collective-permute-start | bytes 393224 | tf_op jit(solution)/shard_map/while/body/eval_jaxpr/ppermute | solution.py:42
  119.3 16.7 %collective-permute-start.1 = (bf16[4,16,1024]{2,1,0:T(8,128)(2,1)}, bf16[4,16,1024]{2,1,0:T(8,128)(2,1)}, u32[]{:S(2)}, u32[]{:S(2)}) collective-permute-start(bf16[4,16,1024]{2,1,0:T(8,128)(2,1)} %get-tuple-element.2976), channel_id=1, source_target_pairs={{0,1},{1,2},{2,3},{3,4},{4,5},{5,6},{6,7},{7,8},{8,9},{9,10},{10,1... | collective-permute-start | bytes 393224 | tf_op jit(solution)/shard_map/while/body/eval_jaxpr/ppermute | solution.py:41
  169.2 14.1 %collective-permute-start.13 = (bf16[2,8,16,512]{3,2,1,0:T(8,128)(2,1)}, bf16[2,8,16,512]{3,2,1,0:T(8,128)(2,1)}, u32[]{:S(2)}, u32[]{:S(2)}) collective-permute-start(bf16[2,8,16,512]{3,2,1,0:T(8,128)(2,1)} %get-tuple-element.3200), channel_id=1, source_target_pairs={{0,32},{32,0},{1,33},{33,1},{2,34},{34,2},{3,35},{35,3},{4,36},{36... | collective-permute-start | bytes 786440 | tf_op jit(solution)/shard_map/ppermute | solution.py:48
  186.5 17.1 %collective-permute-start.2 = (bf16[4,16,1024]{2,1,0:T(8,128)(2,1)}, bf16[4,16,1024]{2,1,0:T(8,128)(2,1)}, u32[]{:S(2)}, u32[]{:S(2)}) collective-permute-start(bf16[4,16,1024]{2,1,0:T(8,128)(2,1)} %get-tuple-element.3006), channel_id=1, source_target_pairs={{1,0},{2,1},{3,2},{4,3},{5,4},{6,5},{7,6},{8,7},{9,8},{10,9},{11,1... | collective-permute-start | bytes 393224 | tf_op jit(solution)/shard_map/while/body/eval_jaxpr/ppermute | solution.py:42
  187.8 15.9 %collective-permute-start.3 = (bf16[4,16,1024]{2,1,0:T(8,128)(2,1)}, bf16[4,16,1024]{2,1,0:T(8,128)(2,1)}, u32[]{:S(2)}, u32[]{:S(2)}) collective-permute-start(bf16[4,16,1024]{2,1,0:T(8,128)(2,1)} %get-tuple-element.3007), channel_id=1, source_target_pairs={{0,1},{1,2},{2,3},{3,4},{4,5},{5,6},{6,7},{7,8},{8,9},{9,10},{10,1... | collective-permute-start | bytes 393224 | tf_op jit(solution)/shard_map/while/body/eval_jaxpr/ppermute | solution.py:41
  213.9 17.1 %collective-permute-start.2 = (bf16[4,16,1024]{2,1,0:T(8,128)(2,1)}, bf16[4,16,1024]{2,1,0:T(8,128)(2,1)}, u32[]{:S(2)}, u32[]{:S(2)}) collective-permute-start(bf16[4,16,1024]{2,1,0:T(8,128)(2,1)} %get-tuple-element.3006), channel_id=1, source_target_pairs={{1,0},{2,1},{3,2},{4,3},{5,4},{6,5},{7,6},{8,7},{9,8},{10,9},{11,1... | collective-permute-start | bytes 393224 | tf_op jit(solution)/shard_map/while/body/eval_jaxpr/ppermute | solution.py:42
  215.2 15.9 %collective-permute-start.3 = (bf16[4,16,1024]{2,1,0:T(8,128)(2,1)}, bf16[4,16,1024]{2,1,0:T(8,128)(2,1)}, u32[]{:S(2)}, u32[]{:S(2)}) collective-permute-start(bf16[4,16,1024]{2,1,0:T(8,128)(2,1)} %get-tuple-element.3007), channel_id=1, source_target_pairs={{0,1},{1,2},{2,3},{3,4},{4,5},{5,6},{6,7},{7,8},{8,9},{9,10},{10,1... | collective-permute-start | bytes 393224 | tf_op jit(solution)/shard_map/while/body/eval_jaxpr/ppermute | solution.py:41
  243.5 11.9 %collective-permute-start.6 = (bf16[4,16,1024]{2,1,0:T(8,128)(2,1)}, bf16[4,16,1024]{2,1,0:T(8,128)(2,1)}, u32[]{:S(2)}, u32[]{:S(2)}) collective-permute-start(bf16[4,16,1024]{2,1,0:T(8,128)(2,1)} %get-tuple-element.3072), channel_id=1, source_target_pairs={{0,1},{1,2},{2,3},{3,4},{4,5},{5,6},{6,7},{7,8},{8,9},{9,10},{10,1... | collective-permute-start | bytes 393224 | tf_op jit(solution)/shard_map/while/body/eval_jaxpr/ppermute | solution.py:41
  248.3 8.4 collective-permute-start.7
  273.1 14.1 %collective-permute-start.6 = (bf16[4,16,1024]{2,1,0:T(8,128)(2,1)}, bf16[4,16,1024]{2,1,0:T(8,128)(2,1)}, u32[]{:S(2)}, u32[]{:S(2)}) collective-permute-start(bf16[4,16,1024]{2,1,0:T(8,128)(2,1)} %get-tuple-element.3072), channel_id=1, source_target_pairs={{0,1},{1,2},{2,3},{3,4},{4,5},{5,6},{6,7},{7,8},{8,9},{9,10},{10,1... | collective-permute-start | bytes 393224 | tf_op jit(solution)/shard_map/while/body/eval_jaxpr/ppermute | solution.py:41
  279.8 7.4 collective-permute-start.7
  299.6 144.6 %collective-permute-start.14 = (bf16[2,8,16,512]{3,2,1,0:T(8,128)(2,1)}, bf16[2,8,16,512]{3,2,1,0:T(8,128)(2,1)S(1)}, u32[]{:S(2)}, u32[]{:S(2)}) collective-permute-start(bf16[2,8,16,512]{3,2,1,0:T(8,128)(2,1)} %get-tuple-element.2101), channel_id=1, source_target_pairs={{0,32},{32,0},{1,33},{33,1},{2,34},{34,2},{3,35},{35,3},{4,36},{36... | collective-permute-start | bytes 786440 | tf_op jit(solution)/shard_map/ppermute | solution.py:48
  445.0 43.4 %copy-start.10 = (f32[512,512]{1,0:T(8,128)S(1)}, f32[512,512]{1,0:T(8,128)}, u32[]{:S(2)}) copy-start(f32[512,512]{1,0:T(8,128)} %get-tuple-element.3359) | copy-start | bytes 3145732 | tf_op jit(solution)/shard_map/while
  480.9 10.3 %collective-permute-start.4 = (bf16[4,16,1024]{2,1,0:T(8,128)(2,1)S(1)}, bf16[4,16,1024]{2,1,0:T(8,128)(2,1)}, u32[]{:S(2)}, u32[]{:S(2)}) collective-permute-start(bf16[4,16,1024]{2,1,0:T(8,128)(2,1)S(1)} %get-tuple-element.3040), channel_id=1, source_target_pairs={{0,1},{1,2},{2,3},{3,4},{4,5},{5,6},{6,7},{7,8},{8,9},{9,10},{10,1... | collective-permute-start | bytes 393224 | tf_op jit(solution)/shard_map/while/body/eval_jaxpr/ppermute | solution.py:41
  487.1 7.0 collective-permute-start.5
  511.2 41.3 %copy-start.10 = (f32[512,512]{1,0:T(8,128)S(1)}, f32[512,512]{1,0:T(8,128)}, u32[]{:S(2)}) copy-start(f32[512,512]{1,0:T(8,128)} %get-tuple-element.3359) | copy-start | bytes 3145732 | tf_op jit(solution)/shard_map/while
  547.1 8.2 collective-permute-start.4
  551.2 8.1 collective-permute-start.5
  577.8 66.3 %reduce-scatter.7.cloned.1.call-start = ((), (), s32[]{:S(2)}) async-start(), calls=%async_computation.5 | async-start | bytes 1310720 | tf_op jit(solution)/shard_map/reduce_scatter | solution.py:342
  580.7 94.5 %reduce-scatter.9.cloned.1.call-start = ((), (), s32[]{:S(2)}) async-start(), calls=%async_computation.6 | async-start | bytes 1966080 | tf_op jit(solution)/shard_map/reduce_scatter | solution.py:345
  582.1 118.4 %reduce-scatter.13.cloned.1.call-start = ((), (), s32[]{:S(2)}) async-start(), calls=%async_computation.8 | async-start | bytes 163840
  583.0 271.6 %all-reduce.11.cloned.1.call-start = ((), (), s32[]{:S(2)}) async-start(), calls=%async_computation.9 | async-start | bytes 1572864 | tf_op jit(solution)/shard_map/psum | solution.py:356
  (70 other events, 349.3 us)
Sparse Core Ops, SparseCore 0:
  9.8 30.4 all-gather.1
  577.9 37.5 reduce-scatter.10
  618.1 25.9 reduce-scatter.6
  646.6 28.4 reduce-scatter.8
  678.2 22.2 reduce-scatter.12
  704.0 150.5 all-reduce.10
